TPU v7x, 512 devices: a whole 4x8x8 slice. The times are simulated.
512 devices in a mesh: dp: 32 (over x_lo, z, core), tensor: 16 (over y, x_hi).
Axes of the slice: x: 4 (x_hi: 2, x_lo: 2; x = x_hi * 2 + x_lo), y: 8, z: 8, core: 2. Of those that a mesh axis runs over, the one named last changes fastest.
Arguments:
- teacher_hidden: bfloat16 [65536, 8192], P('dp', 'tensor'), may hold values from -6 to 6
- teacher_gain: bfloat16 [8192], P('tensor'), may hold values from 0.5 to 1.5
- student_hidden: bfloat16 [65536, 2048], P(('dp', 'tensor')), may hold values from -6 to 6
- student_gain: float32 [2048], replicated, may hold values from 0.5 to 1.5
- projection: bfloat16 [2048, 8192], P('dp', 'tensor'), may hold values from -0.125 to 0.125
- lengths: int32 [32], P('dp'), may hold values from 1 to 2048, as said below
Outputs:
- loss: float32 [], replicated
- grad_gain: float32 [2048], replicated
- grad_proj: float32 [2048, 8192], P('dp', 'tensor')
Inputs may be any that keep to these rules, and one draw needn't show every extreme that they name: `lengths`: one sequence has exactly 2048 valid positions.
All inputs are finite; a program needn't handle non-finite values.
Results may differ from a plain program's by a relative error of at most 0.002.
Values may be sent and summed in bfloat16 or wider, within the bound.
No kernel may reach another device: no remote copies, remote signals or barrier semaphores. Data moves between devices by JAX's collectives and lax.ppermute only.
A program may use at most 64 MiB of HBM per device.

v0:
```python
import jax
import jax.numpy as jnp
from jax import lax
from jax.sharding import PartitionSpec as P

TW = 8192
epsilon = 1e-06


def on_device(teacher_hidden, teacher_gain, student_hidden, student_gain, projection, lengths):
    hidden_f = teacher_hidden.astype(jnp.float32)
    row_squares = lax.psum(jnp.sum(hidden_f * hidden_f, axis=1), "tensor")
    target = (
        hidden_f * lax.rsqrt(row_squares[:, None] / TW + epsilon) * teacher_gain.astype(jnp.float32)
    )
    count = lax.psum(lengths.astype(jnp.float32), "dp")[0]
    student_f = student_hidden.astype(jnp.float32)
    normed = student_f * lax.rsqrt(jnp.mean(student_f * student_f, axis=1, keepdims=True) + epsilon)
    scaled = (normed * student_gain).astype(jnp.bfloat16)
    proj_full = lax.all_gather(projection, "dp", axis=0, tiled=True)
    length_here = lengths[0]
    factor = 2.0 / count
    block_rows = lax.all_gather(scaled, "tensor", axis=0, tiled=True)
    row_count = block_rows.shape[0]
    predicted = jnp.dot(block_rows, proj_full, preferred_element_type=jnp.float32)
    positions = jnp.arange(row_count, dtype=jnp.int32)
    valid = positions < length_here
    diff = jnp.where(valid[:, None], predicted - target, jnp.float32(0.0))
    slope = (diff * factor).astype(jnp.bfloat16)
    grad_total = jnp.dot(block_rows.T, slope, preferred_element_type=jnp.float32)
    loss_part = jnp.sum(diff * diff)
    grad_proj = lax.psum_scatter(grad_total, "dp", scatter_dimension=0, tiled=True)
    gain_part = jnp.sum(proj_full.astype(jnp.float32) * grad_total, axis=1)
    loss_all, gain_all = lax.psum((loss_part, gain_part), ("dp", "tensor"))
    loss = loss_all / (count * TW)
    grad_gain = gain_all / student_gain
    return (loss, grad_gain, grad_proj)


def solution(mesh):
    return jax.shard_map(
        on_device,
        mesh=mesh,
        in_specs=(
            P("dp", "tensor"),
            P("tensor"),
            P(("dp", "tensor"), None),
            P(),
            P("dp", "tensor"),
            P("dp"),
        ),
        out_specs=(P(), P(), P("dp", "tensor")),
        check_vma=False,
    )
```

profile of v0, /device:TPU:8, one launch (start us, length us, event | category | flops | bytes accessed | tf_op | source)
XLA Modules:
  0.0 378.2 jit_solution(16109726886987439591)
XLA Ops:
  7.2 0.0 all-gather.5.cloned.1.call-start
  7.2 0.7 all-gather.5.cloned.1.call-update
  7.9 0.0 copy-start
  7.9 0.0 all-gather.3.cloned.1.call-start
  8.0 1.4 fusion.6
  9.3 2.1 fusion.8
  11.4 0.0 all-gather.3.cloned.1.call-update
  11.4 0.0 reduce-scatter.4.cloned.1.call-start
  12.1 62.9 %psum.30 = f32[1]{0:T(128)} all-reduce(f32[1]{0:T(128)S(6)} %convert_element_type.25), channel_id=1, replica_groups=mesh['dp'=32,'tensor'=16] {'dp'}, use_global_device_ids=true, to_apply=%region_5.6 | all-reduce | flops 1 | bytes 8 | tf_op jit(solution)/shard_map/psum | solution.py:16
  75.0 0.7 convert_element_type.24
  76.4 2.1 fusion
  78.5 40.7 %psum.28 = f32[2048]{0:T(1024)S(1)} all-reduce(f32[2048]{0:T(1024)S(1)} %fusion), channel_id=1, replica_groups=mesh['dp'=32,'tensor'=16] {'tensor'}, use_global_device_ids=true, to_apply=%region_2.0 | all-reduce | flops 2048 | bytes 16384 | tf_op jit(solution)/shard_map/psum | solution.py:12
  119.3 0.0 all-gather.5.cloned.1.call-done
  119.3 4.0 %copy.11 = bf16[2048,512]{0,1:T(8,128)(2,1)} copy(bf16[2048,512]{1,0:T(8,128)(2,1)} %all-gather.5.cloned.1.call-done) | data formatting | bytes 4194304 | tf_op jit(solution)/shard_map/all_gather | solution.py:20
  123.2 101.4 %all-gather.3.cloned.1.call-done = bf16[2048,2048]{1,0:T(8,128)(2,1)} async-done(((bf16[128,2048]{1,0:T(8,128)(2,1)}), bf16[2048,2048]{1,0:T(8,128)(2,1)}) %all-gather.3.cloned.1.call-update) | async-done | bytes 8388624 | tf_op jit(solution)/shard_map/all_gather | solution.py:23
  224.6 0.0 copy-done
  224.6 9.7 %multiply_reduce_fusion.1 = (f32[]{:T(128)}, f32[2048,512]{1,0:T(8,128)S(1)}) fusion(f32[512]{0:T(512)S(1)} %convert_element_type.24, f32[2048]{0:T(1024)S(1)} %add_rsqrt_fusion, bf16[2048,512]{1,0:T(8,128)(2,1)S(1)} %copy-done, bf16[2048,2048]{1,0:T(8,128)(2,1)} %all-gather.3.cloned.1.call-done, bf16[2048,512]{1,0:T(8,128)(2,1)} %all-gather.5.cloned.1.call-done, ...), kind=kOutput, calls=%fused_computation.8 | convolution fusion | flops 4302307328 | bytes 16789508 | tf_op jit(solution)/shard_map/dot_general | solution.py:25
  234.3 0.0 copy-done.3
  234.3 6.3 %multiply_reduce_fusion = (f32[2048]{0:T(1024)S(1)}, f32[2048,512]{0,1:T(8,128)}) fusion(bf16[2048,512]{0,1:T(8,128)(2,1)S(1)} %copy-done.1, bf16[2048,2048]{1,0:T(8,128)(2,1)S(1)} %copy-done.3, f32[2048,512]{1,0:T(8,128)S(1)} %get-tuple-element.12, f32[]{:T(128)} %bitcast.2), kind=kOutput, calls=%fused_computation.6 | convolution fusion | flops 4300208128 | bytes 18882564 | tf_op jit(solution)/shard_map/dot_general | solution.py:30
  240.5 5.3 %copy.13 = f32[2048,512]{1,0:T(8,128)} copy(f32[2048,512]{0,1:T(8,128)} %get-tuple-element.14) | data formatting | bytes 8388608
  245.9 0.0 reduce-scatter.4.cloned.1.call-update
  246.5 97.7 %all-reduce = (f32[]{:T(128)}, f32[2048]{0:T(1024)S(1)}) all-reduce(f32[]{:T(128)} %get-tuple-element.11, f32[2048]{0:T(1024)S(1)} %get-tuple-element.13), channel_id=1, replica_groups=mesh['dp'=32,'tensor'=16] {'dp','tensor'}, use_global_device_ids=true, to_apply=%region_4.5 | all-reduce | flops 2049 | bytes 16392 | tf_op jit(solution)/shard_map/psum | solution.py:34
  344.3 0.6 div.31
  345.6 25.0 %reduce-scatter.4.cloned.1.call-done = f32[64,512]{1,0:T(8,128)} async-done(((f32[2048,512]{1,0:T(8,128)}), f32[64,512]{1,0:T(8,128)}) %reduce-scatter.4.cloned.1.call-update) | async-done | bytes 131088
  (8 shorter events, 0.0 us)
Async XLA Ops:
  7.2 112.1 %all-gather.5.cloned.1.call-start = ((), (), s32[]{:S(2)}) async-start(), calls=%async_computation.2 | async-start | bytes 2162688 | tf_op jit(solution)/shard_map/all_gather | solution.py:20
  7.9 216.7 %copy-start = (bf16[2048,512]{1,0:T(8,128)(2,1)S(1)}, bf16[2048,512]{1,0:T(8,128)(2,1)}, u32[]{:S(2)}) copy-start(bf16[2048,512]{1,0:T(8,128)(2,1)} %param.6) | copy-start | bytes 6291460
  7.9 216.7 %all-gather.3.cloned.1.call-start = ((), (), s32[]{:S(2)}) async-start(), calls=%async_computation.1 | async-start | bytes 8912896 | tf_op jit(solution)/shard_map/all_gather | solution.py:23
  11.4 359.1 %reduce-scatter.4.cloned.1.call-start = ((), (), s32[]{:S(2)}) async-start(), calls=%async_computation.3 | async-start | bytes 4325376
  224.6 9.7 %copy-start.1 = (bf16[2048,512]{0,1:T(8,128)(2,1)S(1)}, bf16[2048,512]{0,1:T(8,128)(2,1)}, u32[]{:S(2)}) copy-start(bf16[2048,512]{0,1:T(8,128)(2,1)} %copy.11) | copy-start | bytes 6291460
  224.6 9.7 %copy-start.3 = (bf16[2048,2048]{1,0:T(8,128)(2,1)S(1)}, bf16[2048,2048]{1,0:T(8,128)(2,1)}, u32[]{:S(2)}) copy-start(bf16[2048,2048]{1,0:T(8,128)(2,1)} %all-gather.3.cloned.1.call-done) | copy-start | bytes 25165828
  245.9 98.4 %copy-start.2 = (f32[2048]{0:T(1024)S(1)}, f32[2048]{0:T(1024)}, u32[]{:S(2)}) copy-start(f32[2048]{0:T(1024)} %param.9) | copy-start | bytes 24580
Sparse Core Ops, SparseCore 0:
  10.1 72.4 all-gather.4
  85.8 138.7 all-gather.2
  246.0 124.4 reduce-scatter.3
where the time goes:
time: 379 us; the launch traced here: 378 us
  blocking collectives  201 us (53%)
  waiting for transfers between devices  127 us (34%)
  between operations  17.6 us (5%)
  matrix products  15.9 us (4%)
  local copies, waits for them, and re-layouts  9.33 us (2%)
  other arithmetic  6.84 us (2%)
    all_gather x1, waiting for transfers between devices, on_device(): block_rows = lax.all_gather(scaled, 'tensor', axis=0, tiled=True)  101 us
    psum x1, blocking collectives, on_device(): loss_all, gain_all = lax.psum((loss_part, gain_part), ('dp', 'tensor'))  97.7 us
    psum x1, blocking collectives, on_device(): count = lax.psum(lengths.astype(jnp.float32), 'dp')[0]  62.9 us
    psum x1, blocking collectives, on_device(): row_squares = lax.psum(jnp.sum(hidden_f * hidden_f, axis=1), 'tensor')  40.7 us
    unnamed x4, waiting for transfers between devices  25.7 us
    dot_general x1, matrix products, on_device(): jnp.dot(block_rows, proj_full, preferred_element_type=jnp.float32)  9.66 us
  transfers between devices with their start and end apart: 3, of which 2 were waited for; matrix products, arithmetic and copies ran while one was open for 3% of the time, Pallas kernels for 0%

commit v1 on v0

--- a/solution.py
+++ b/solution.py
@@ -20,7 +20,9 @@
     proj_full = lax.all_gather(projection, "dp", axis=0, tiled=True)
     length_here = lengths[0]
     factor = 2.0 / count
-    block_rows = lax.all_gather(scaled, "tensor", axis=0, tiled=True)
+    block_rows = jnp.concatenate(
+        lax.all_to_all(jnp.stack([scaled] * lax.axis_size("tensor")), "tensor", 0, 0), axis=0
+    )
     row_count = block_rows.shape[0]
     predicted = jnp.dot(block_rows, proj_full, preferred_element_type=jnp.float32)
     positions = jnp.arange(row_count, dtype=jnp.int32)

time: 379 us -> 412 us (1.087)
  blocking collectives: 201 us -> 321 us
  waiting for transfers between devices: 127 us -> 26.2 us
  starting transfers between devices: 0.12 us -> 10.5 us
  local copies, waits for them, and re-layouts: 9.33 us -> 13.6 us
    psum x1, blocking collectives: 40.7 us -> 153 us  [on_device(): row_squares = lax.psum(jnp.sum(hidden_f * hidden_f, axis=1), 'tensor')]
    all_gather x1 -> x0, waiting for transfers between devices: 101 us -> none  [on_device(): block_rows = lax.all_gather(scaled, 'tensor', axis=0, tiled=True)]
    all_to_all x0 -> x1, starting transfers between devices: none -> 10.4 us  [on_device(): lax.all_to_all(jnp.stack([scaled] * lax.axis_size('tensor')), 'tensor', 0...]
    psum x1, blocking collectives: 97.7 us -> 103 us  [on_device(): loss_all, gain_all = lax.psum((loss_part, gain_part), ('dp', 'tensor'))]
    another operation x0 -> x1, local copies, waits for them, and re-layouts: none -> 4.28 us  [on_device(): jnp.stack([scaled] * lax.axis_size('tensor'))]
    unnamed x4 -> x3, waiting for transfers between devices: 25.7 us -> 26.2 us
  transfers between devices with their start and end apart: 3 -> 3, of which waited for: 2 -> 1; matrix products, arithmetic and copies ran while one was open for 3% -> 1% of each run, Pallas kernels for 0% -> 0%
where the time goes in v1:
time: 412 us; the launch traced here: 411 us
  blocking collectives  321 us (78%)
  waiting for transfers between devices  26.2 us (6%)
  matrix products  18.7 us (5%)
  between operations  17.9 us (4%)
  local copies, waits for them, and re-layouts  13.6 us (3%)
  starting transfers between devices  10.5 us (3%)
    psum x1, blocking collectives, on_device(): row_squares = lax.psum(jnp.sum(hidden_f * hidden_f, axis=1), 'tensor')  153 us
    psum x1, blocking collectives, on_device(): loss_all, gain_all = lax.psum((loss_part, gain_part), ('dp', 'tensor'))  103 us
    psum x1, blocking collectives, on_device(): count = lax.psum(lengths.astype(jnp.float32), 'dp')[0]  64.5 us
    unnamed x3, waiting for transfers between devices  26.2 us
    all_to_all x1, starting transfers between devices, on_device(): lax.all_to_all(jnp.stack([scaled] * lax.axis_size('tensor')), 'tensor', 0...  10.4 us
    dot_general x1, matrix products, on_device(): jnp.dot(block_rows.T, slope, preferred_element_type=jnp.float32)  9.52 us
    dot_general x1, matrix products, on_device(): jnp.dot(block_rows, proj_full, preferred_element_type=jnp.float32)  9.19 us
  transfers between devices with their start and end apart: 3, of which 1 were waited for; matrix products, arithmetic and copies ran while one was open for 1% of the time, Pallas kernels for 0%

profile of v1, /device:TPU:8, one launch (start us, length us, event | category | flops | bytes accessed | tf_op | source)
XLA Modules:
  0.0 411.3 jit_solution(13699958672595917827)
XLA Ops:
  7.2 1.2 fusion.6
  8.4 1.2 fusion.8
  9.6 4.3 %stack.2 = bf16[16,128,2048]{2,1,0:T(8,128)(2,1)} broadcast(bf16[128,2048]{1,0:T(8,128)(2,1)S(1)} %fusion.8), dimensions={1,2} | broadcast | bytes 8912896 | tf_op jit(solution)/shard_map/stack | solution.py:24
  13.9 10.4 %all-to-all-start = ((bf16[16,128,2048]{2,1,0:T(8,128)(2,1)}), bf16[16,128,2048]{2,1,0:T(8,128)(2,1)}, u32[]{:S(2)}, u32[]{:S(2)}) async-start(bf16[16,128,2048]{2,1,0:T(8,128)(2,1)} %stack.2), calls=%async_computation | async-start | bytes 16777216 | tf_op jit(solution)/shard_map/all_to_all | solution.py:24
  24.4 0.0 all-gather.2.cloned.1.call-start
  24.4 0.7 all-gather.2.cloned.1.call-update
  25.1 0.0 reduce-scatter.4.cloned.1.call-start
  25.8 64.5 %psum.30 = f32[1]{0:T(128)} all-reduce(f32[1]{0:T(128)S(6)} %convert_element_type.25), channel_id=1, replica_groups=mesh['dp'=32,'tensor'=16] {'dp'}, use_global_device_ids=true, to_apply=%region_5.6 | all-reduce | flops 1 | bytes 8 | tf_op jit(solution)/shard_map/psum | solution.py:16
  90.3 0.0 copy-done.3
  91.0 0.0 copy-done
  91.0 0.5 fusion
  91.4 152.9 %psum.28 = f32[2048]{0:T(1024)S(1)} all-reduce(f32[2048]{0:T(1024)S(1)} %fusion), channel_id=1, replica_groups=mesh['dp'=32,'tensor'=16] {'tensor'}, use_global_device_ids=true, to_apply=%region_2.0 | all-reduce | flops 2048 | bytes 16384 | tf_op jit(solution)/shard_map/psum | solution.py:12
  244.4 0.0 all-gather.2.cloned.1.call-done
  244.5 4.0 copy.11
  248.4 0.0 all-to-all-done
  248.4 9.2 %multiply_reduce_fusion.1 = (f32[]{:T(128)}, f32[2048,512]{1,0:T(8,128)S(1)}) fusion(f32[512]{0:T(512)S(1)} %convert_element_type.24, f32[2048]{0:T(1024)S(1)} %add_rsqrt_fusion, bf16[2048,512]{1,0:T(8,128)(2,1)S(1)} %copy-done, bf16[2048,2048]{1,0:T(8,128)(2,1)} %bitcast.1, bf16[2048,512]{1,0:T(8,128)(2,1)} %all-gather.2.cloned.1.call-done, ...), kind=kOutput, calls=%fused_computation.8 | convolution fusion | flops 4302307328 | bytes 16789508 | tf_op jit(solution)/shard_map/dot_general | solution.py:27
  257.6 0.0 copy-done.1
  257.6 9.5 %multiply_reduce_fusion = (f32[2048]{0:T(1024)S(1)}, f32[2048,512]{0,1:T(8,128)}) fusion(bf16[2048,512]{0,1:T(8,128)(2,1)S(1)} %copy-done.1, bf16[2048,2048]{1,0:T(8,128)(2,1)} %bitcast.1, f32[2048,512]{1,0:T(8,128)S(1)} %get-tuple-element.12, f32[]{:T(128)} %bitcast.3), kind=kOutput, calls=%fused_computation.6 | convolution fusion | flops 4300208128 | bytes 18882564 | tf_op jit(solution)/shard_map/dot_general | solution.py:32
  267.1 5.3 %copy.13 = f32[2048,512]{1,0:T(8,128)} copy(f32[2048,512]{0,1:T(8,128)} %get-tuple-element.14) | data formatting | bytes 8388608
  272.5 0.0 reduce-scatter.4.cloned.1.call-update
  273.2 103.4 %all-reduce = (f32[]{:T(128)}, f32[2048]{0:T(1024)S(1)}) all-reduce(f32[]{:T(128)} %get-tuple-element.11, f32[2048]{0:T(1024)S(1)} %get-tuple-element.13), channel_id=1, replica_groups=mesh['dp'=32,'tensor'=16] {'dp','tensor'}, use_global_device_ids=true, to_apply=%region_4.5 | all-reduce | flops 2049 | bytes 16392 | tf_op jit(solution)/shard_map/psum | solution.py:36
  376.6 0.0 copy-done.2
  376.6 0.6 div.31
  377.9 25.5 %reduce-scatter.4.cloned.1.call-done = f32[64,512]{1,0:T(8,128)} async-done(((f32[2048,512]{1,0:T(8,128)}), f32[64,512]{1,0:T(8,128)}) %reduce-scatter.4.cloned.1.call-update) | async-done | bytes 131088
  (8 shorter events, 0.0 us)
Async XLA Ops:
  13.9 76.3 %copy-start.3 = (bf16[512]{0:T(512)(128)(2,1)S(1)}, bf16[512]{0:T(512)(128)(2,1)}, u32[]{:S(2)}) copy-start(bf16[512]{0:T(512)(128)(2,1)} %param.7) | copy-start | bytes 3076
  13.9 77.0 %copy-start = (bf16[2048,512]{1,0:T(8,128)(2,1)S(1)}, bf16[2048,512]{1,0:T(8,128)(2,1)}, u32[]{:S(2)}) copy-start(bf16[2048,512]{1,0:T(8,128)(2,1)} %param.6) | copy-start | bytes 6291460
  13.9 234.5 %all-to-all-start = ((bf16[16,128,2048]{2,1,0:T(8,128)(2,1)}), bf16[16,128,2048]{2,1,0:T(8,128)(2,1)}, u32[]{:S(2)}, u32[]{:S(2)}) async-start(bf16[16,128,2048]{2,1,0:T(8,128)(2,1)} %stack.2), calls=%async_computation | async-start | bytes 16777216 | tf_op jit(solution)/shard_map/all_to_all | solution.py:24
  24.4 220.1 %all-gather.2.cloned.1.call-start = ((), (), s32[]{:S(2)}) async-start(), calls=%async_computation.2 | async-start | bytes 2162688 | tf_op jit(solution)/shard_map/all_gather | solution.py:20
  25.1 378.3 %reduce-scatter.4.cloned.1.call-start = ((), (), s32[]{:S(2)}) async-start(), calls=%async_computation.3 | async-start | bytes 4325376
  248.4 9.2 %copy-start.1 = (bf16[2048,512]{0,1:T(8,128)(2,1)S(1)}, bf16[2048,512]{0,1:T(8,128)(2,1)}, u32[]{:S(2)}) copy-start(bf16[2048,512]{0,1:T(8,128)(2,1)} %copy.11) | copy-start | bytes 6291460
  272.5 104.1 %copy-start.2 = (f32[2048]{0:T(1024)S(1)}, f32[2048]{0:T(1024)}, u32[]{:S(2)}) copy-start(f32[2048]{0:T(1024)} %param.9) | copy-start | bytes 24580
Sparse Core Ops, SparseCore 0:
  27.3 71.7 all-gather.1
  272.6 130.6 reduce-scatter.3
